TPU v7x, 128 devices: a whole 4x4x4 slice. The times are simulated.
128 devices in a mesh: slab: 4 (over y_lo, core), pencil: 32 (over x, z, y_hi).
Axes of the slice: x: 4, y: 4 (y_hi: 2, y_lo: 2; y = y_hi * 2 + y_lo), z: 4, core: 2. Of those that a mesh axis runs over, the one named last changes fastest.
Arguments:
- density: float32 [16, 256, 4096], P('slab', 'pencil'), parts along dimension 0, may hold values from 0.5 to 2
- velocity: float32 [2, 16, 256, 4096], P(None, 'slab', 'pencil'), parts along dimension 1, may hold values from -2.5 to 2.5
- pressure: float32 [16, 256, 4096], P('slab', 'pencil'), parts along dimension 0, may hold values from 0.5 to 2
Outputs:
- new_density: float32 [16, 256, 4096], P('slab', 'pencil'), parts along dimension 0
- new_velocity: float32 [2, 16, 256, 4096], P(None, 'slab', 'pencil'), parts along dimension 1
- new_pressure: float32 [16, 256, 4096], P('slab', 'pencil'), parts along dimension 0
There are 4 independent parts, one for each index of `slab`. A program takes and returns all parts, laid end to end along the dimension named above; each array names one. Nothing has to cross between parts.
All inputs are finite; a program needn't handle non-finite values.
Results may differ from a plain program's by a relative error of at most 0.00002.
Values sent between devices are 32-bit elements; how exact they have to be, the bound alone decides.
A program may use at most 64 MiB of HBM per device.

v0:
```python
import jax
import jax.numpy as jnp
from jax import lax
from jax.experimental import pallas as pl
from jax.experimental.pallas import tpu as pltpu
from jax.sharding import PartitionSpec as P

MESH = pl.DeviceIdType.MESH
NEWTON = 4
LANES = 128
ROWS = 8
QUARTER = 8
HALO = 3
GROUP = 3


def inverse(value):
    return pl.reciprocal(value, approx=False)


def column_shift(values, step):
    lane = lax.broadcasted_iota(jnp.int32, values.shape, 2)
    if step == 1:
        turned = pltpu.roll(values, LANES - 1, 2)
        other = jnp.concatenate([turned[1:], turned[-1:]], axis=0)
        return jnp.where(lane == LANES - 1, other, turned)
    turned = pltpu.roll(values, 1, 2)
    other = jnp.concatenate([turned[:1], turned[:-1]], axis=0)
    return jnp.where(lane == 0, other, turned)


def limited(values, dr, dl):
    two_r = 2.0 * jnp.abs(dr)
    two_l = 2.0 * jnp.abs(dl)
    left = values + jnp.minimum(jnp.maximum(dr, -two_l), two_l)
    right = values + jnp.minimum(jnp.maximum(dl, -two_r), two_r)
    return left, right


def half_step(d, d_before, d_after):
    raw = 0.5 * d + (d_before - d_after) * (1.0 / 12.0)
    return jnp.minimum(jnp.maximum(raw, jnp.minimum(d, 0.0)), jnp.maximum(d, 0.0))


def edges_along_columns(values):
    d = column_shift(values, 1) - values
    dr = half_step(d, column_shift(d, -1), column_shift(d, 1))
    dl = column_shift(dr - d, -1)
    left, right = limited(values, dr, dl)
    return left[:-1], column_shift(right, 1)[:-1]


def edges_along_rows(values):
    d = values[1:] - values[:-1]
    dr = half_step(d[1:-1], d[:-2], d[2:])
    back = dr - d[1:-1]
    left, right = limited(values[2:12], dr[1:], back[:-1])
    return left[:-1], right[1:]


def fluxes(left, right, ratio):
    rho_l, un_l, ut_l, p_l = left
    rho_r, un_r, ut_r, p_r = right
    b_l = 0.2 * rho_l * p_l
    b_r = 0.2 * rho_r * p_r
    a_l = 1.2 * rho_l
    a_r = 1.2 * rho_r
    c_l = 3.5 * b_l
    c_r = 3.5 * b_r
    du = un_l - un_r
    inv_l = lax.rsqrt(7.0 * b_l)
    inv_r = lax.rsqrt(7.0 * b_r)
    floor_p = 0.1 * jnp.minimum(p_l, p_r)
    pstar = (p_l * inv_l + p_r * inv_r + du) * inverse(inv_l + inv_r)
    pstar = jnp.maximum(pstar, floor_p)
    for _ in range(NEWTON):
        s_l = lax.rsqrt(a_l * pstar + b_l)
        s_r = lax.rsqrt(a_r * pstar + b_r)
        slope = s_l * (0.5 + c_l * (s_l * s_l)) + s_r * (0.5 + c_r * (s_r * s_r))
        gap = (pstar - p_l) * s_l + (pstar - p_r) * s_r - du
        pstar = jnp.maximum(pstar - gap * inverse(slope), floor_p)
    s_l = lax.rsqrt(a_l * pstar + b_l)
    s_r = lax.rsqrt(a_r * pstar + b_r)
    ustar = 0.5 * ((un_l + un_r) + ((pstar - p_r) * s_r - (pstar - p_l) * s_l))
    from_left = ustar >= 0.0
    rho = jnp.where(from_left, rho_l, rho_r)
    un = jnp.where(from_left, un_l, un_r)
    ut = jnp.where(from_left, ut_l, ut_r)
    p = jnp.where(from_left, p_l, p_r)
    u_r = ratio * ustar
    mass = u_r * rho
    normal = mass * ustar + ratio * pstar
    trans = mass * ut
    energy = u_r * (2.5 * p + pstar) + 0.5 * mass * (un * un + ut * ut)
    return mass, normal, trans, energy


def primitives(rho, mx, my, energy):
    inv = inverse(rho)
    u = mx * inv
    v = my * inv
    p = 0.4 * (energy - 0.5 * (mx * u + my * v))
    return u, v, p


def face_fluxes(edge_ref, flux_ref, ratio):
    for first in range(0, QUARTER + 1, GROUP):
        part = pl.ds(first, GROUP)
        left = tuple(edge_ref[f, 0, part] for f in range(4))
        right = tuple(edge_ref[f, 1, part] for f in range(4))
        for f, flux in enumerate(fluxes(left, right, ratio)):
            flux_ref[f, part] = flux


def kernel(
    density, velocity, pressure, new_density, new_velocity, new_pressure,
    start, first, second, final, edge, flux, to_up, to_down, from_up, from_down,
    in_sem, out_sem, send_sem, recv_sem,
):
    slab = lax.axis_index("slab")
    me = lax.axis_index("pencil")
    count = lax.axis_size("pencil")
    up = lax.rem(me + 1, count)
    down = lax.rem(me + count - 1, count)
    planes, blocks = start.shape[1], start.shape[2]
    quarters = blocks // QUARTER
    units = planes * quarters

    barrier = pltpu.get_barrier_semaphore()
    for neighbour in (up, down):
        pl.semaphore_signal(barrier, inc=1, device_id=(slab, neighbour), device_id_type=MESH)

    def sources(plane):
        return (density.at[plane], velocity.at[0, plane], velocity.at[1, plane], pressure.at[plane])

    def load(plane, f):
        return pltpu.make_async_copy(sources(plane)[f], start.at[f, plane], in_sem.at[f, plane])

    for plane in range(planes):
        for f in range(4):
            load(plane, f).start()

    def around(quarter):
        before = lax.rem(quarter * QUARTER + blocks - 1, blocks)
        after = lax.rem(quarter * QUARTER + QUARTER, blocks)
        return before, quarter * QUARTER, after

    def column_sweep(quarter, read, conserved, write, ratio):
        before, own, after = around(quarter)
        for f in range(4):
            values = jnp.concatenate([read(f, before, 1), read(f, own, QUARTER), read(f, after, 1)], axis=0)
            left, right = edges_along_columns(values)
            edge[f, 0] = left
            edge[f, 1] = right
        face_fluxes(edge, flux, ratio)
        changed = []
        for f, old in enumerate(conserved(own)):
            here = flux[f]
            changed.append(old - (here - column_shift(here, -1))[1:])
        write(own, changed)

    def copy_up(unit):
        return pltpu.make_async_remote_copy(
            to_up.at[unit], from_down.at[unit], send_sem.at[0, unit], recv_sem.at[0, unit],
            device_id=(slab, up), device_id_type=MESH,
        )

    def copy_down(unit):
        return pltpu.make_async_remote_copy(
            to_down.at[unit], from_up.at[unit], send_sem.at[1, unit], recv_sem.at[1, unit],
            device_id=(slab, down), device_id_type=MESH,
        )

    def rows_of(ref, f, plane, block):
        return ref[f, plane, pl.ds(pl.multiple_of(block * ROWS, ROWS), ROWS)]

    def line(quarter, row):
        return pl.ds(quarter * (QUARTER * ROWS) + row, QUARTER, stride=ROWS)

    def first_sweep(unit, carry):
        plane, quarter = unit // quarters, lax.rem(unit, quarters)

        @pl.when(quarter == 0)
        def _():
            for f in range(4):
                load(plane, f).wait()

        def read(f, block, n):
            return start[f, plane, pl.ds(block, n)]

        def conserved(own):
            rho, u, v, p = (read(f, own, QUARTER) for f in range(4))
            mx = rho * u
            my = rho * v
            return rho, mx, my, 2.5 * p + 0.5 * (mx * u + my * v)

        def write(own, changed):
            rho, mx, my, energy = changed
            u, v, p = primitives(rho, mx, my, energy)
            here = pl.ds(pl.multiple_of(own * ROWS, QUARTER * ROWS), QUARTER * ROWS)
            for f, value in enumerate((rho, u, v, p, mx, my, energy)):
                first[f, plane, here] = value.reshape(QUARTER * ROWS, LANES)

        column_sweep(quarter, read, conserved, write, 0.025)
        for f in range(4):
            for row in range(HALO):
                to_up[unit, f * HALO + row] = first[f, plane, line(quarter, ROWS - HALO + row)]
                to_down[unit, f * HALO + row] = first[f, plane, line(quarter, row)]

        @pl.when(unit == 0)
        def _():
            pl.semaphore_wait(barrier, 2)

        copy_up(unit).start()
        copy_down(unit).start()
        return carry

    lax.fori_loop(0, units, first_sweep, 0)

    def row_sweep(unit):
        plane, quarter = unit // quarters, lax.rem(unit, quarters)
        copy_up(unit).wait_recv()
        copy_down(unit).wait_recv()
        for place, f in enumerate((0, 2, 1, 3)):
            values = jnp.concatenate(
                [from_down[unit, pl.ds(f * HALO, HALO)]]
                + [first[f, plane, line(quarter, row)][None] for row in range(ROWS)]
                + [from_up[unit, pl.ds(f * HALO, HALO)]],
                axis=0,
            )
            left, right = edges_along_rows(values)
            edge[place, 0] = left
            edge[place, 1] = right
        face_fluxes(edge, flux, 0.05)
        mass, normal, trans, energy = (flux[f][1:] - flux[f][:-1] for f in range(4))
        rho, mx, my, en = (
            jnp.stack([first[f, plane, line(quarter, row)] for row in range(ROWS)]) for f in (0, 4, 5, 6)
        )
        rho = rho - mass
        mx = mx - trans
        my = my - normal
        en = en - energy
        u, v, p = primitives(rho, mx, my, en)
        for f, value in enumerate((rho, u, v, p, mx, my, en)):
            for row in range(ROWS):
                second[f, plane, line(quarter, row)] = value[row]

    def store(unit, f):
        plane, quarter = unit // quarters, lax.rem(unit, quarters)
        part = pl.ds(quarter * QUARTER, QUARTER)
        target = (
            new_density.at[plane, part], new_velocity.at[0, plane, part],
            new_velocity.at[1, plane, part], new_pressure.at[plane, part],
        )[f]
        return pltpu.make_async_copy(final.at[f, plane, part], target, out_sem.at[f, unit])

    def last_sweep(unit):
        plane, quarter = unit // quarters, lax.rem(unit, quarters)

        def read(f, block, n):
            here = pl.ds(pl.multiple_of(block * ROWS, ROWS), n * ROWS)
            return second[f, plane, here].reshape(n, ROWS, LANES)

        def conserved(own):
            return tuple(read(f, own, QUARTER) for f in (0, 4, 5, 6))

        def write(own, changed):
            rho, mx, my, energy = changed
            u, v, p = primitives(rho, mx, my, energy)
            for f, value in enumerate((rho, u, v, p)):
                final[f, plane, pl.ds(own, QUARTER)] = value

        column_sweep(quarter, read, conserved, write, 0.025)
        for f in range(4):
            store(unit, f).start()

    def later(unit, carry):
        @pl.when(unit < units)
        def _():
            row_sweep(unit)

        @pl.when(unit >= quarters)
        def _():
            last_sweep(unit - quarters)

        return carry

    lax.fori_loop(0, units + quarters, later, 0)

    def finish(unit, carry):
        copy_up(unit).wait_send()
        copy_down(unit).wait_send()
        for f in range(4):
            store(unit, f).wait()
        return carry

    lax.fori_loop(0, units, finish, 0)


def on_device(density, velocity, pressure):
    planes, rows, columns = density.shape
    blocks = columns // LANES
    units = planes * blocks // QUARTER

    def blocked(a):
        lead = a.shape[:-2]
        return jnp.swapaxes(a.reshape(*lead, rows, blocks, LANES), -3, -2)

    def unblocked(a):
        lead = a.shape[:-3]
        return jnp.swapaxes(a, -3, -2).reshape(*lead, rows, columns)

    any_space = pl.BlockSpec(memory_space=pl.ANY)
    shape = (planes, blocks, rows, LANES)
    f32 = jnp.float32
    halo = (units, 4 * HALO, QUARTER, LANES)
    outs = pl.pallas_call(
        kernel,
        out_shape=(
            jax.ShapeDtypeStruct(shape, f32),
            jax.ShapeDtypeStruct((2, *shape), f32),
            jax.ShapeDtypeStruct(shape, f32),
        ),
        in_specs=[any_space] * 3,
        out_specs=(any_space,) * 3,
        scratch_shapes=[
            pltpu.VMEM((4, *shape), f32),
            pltpu.VMEM((7, planes, blocks * rows, LANES), f32),
            pltpu.VMEM((7, planes, blocks * rows, LANES), f32),
            pltpu.VMEM((4, *shape), f32),
            pltpu.VMEM((4, 2, QUARTER + 1, rows, LANES), f32),
            pltpu.VMEM((4, QUARTER + 1, rows, LANES), f32),
            pltpu.VMEM(halo, f32),
            pltpu.VMEM(halo, f32),
            pltpu.VMEM(halo, f32),
            pltpu.VMEM(halo, f32),
            pltpu.SemaphoreType.DMA((4, planes)),
            pltpu.SemaphoreType.DMA((4, units)),
            pltpu.SemaphoreType.DMA((2, units)),
            pltpu.SemaphoreType.DMA((2, units)),
        ],
        compiler_params=pltpu.CompilerParams(
            collective_id=0, has_side_effects=True, vmem_limit_bytes=48 * 2**20
        ),
    )(blocked(density), blocked(velocity), blocked(pressure))
    return tuple(unblocked(a) for a in outs)


def solution(mesh):
    one = P("slab", "pencil", None)
    two = P(None, "slab", "pencil", None)
    return jax.shard_map(on_device, mesh=mesh, in_specs=(one, two, one), out_specs=(one, two, one), check_vma=False)
```

profile of v0, /device:TPU:96, one launch (start us, length us, event | category | flops | bytes accessed | tf_op | source)
XLA Modules:
  0.0 58.3 jit_solution(5216797139001187110)
XLA Ops:
  0.6 0.0 copy-start
  0.6 1.2 %copy-done = f32[2,4,8,4096]{3,2,1,0:T(8,128)S(1)} copy-done((f32[2,4,8,4096]{3,2,1,0:T(8,128)S(1)}, f32[2,4,8,4096]{3,2,1,0:T(8,128)}, u32[]{:S(2)}) %copy-start) | copy-done | bytes 1048600
  1.9 0.0 copy-start.1
  1.9 1.0 %copy-done.1 = f32[4,8,4096]{2,1,0:T(8,128)S(1)} copy-done((f32[4,8,4096]{2,1,0:T(8,128)S(1)}, f32[4,8,4096]{2,1,0:T(8,128)}, u32[]{:S(2)}) %copy-start.1) | copy-done | bytes 524312
  2.9 0.0 copy-start.2
  2.9 1.0 %copy-done.2 = f32[4,8,4096]{2,1,0:T(8,128)S(1)} copy-done((f32[4,8,4096]{2,1,0:T(8,128)S(1)}, f32[4,8,4096]{2,1,0:T(8,128)}, u32[]{:S(2)}) %copy-start.2) | copy-done | bytes 524312
  3.9 51.8 %shard_map.58 = (f32[4,32,8,128]{3,2,1,0:T(8,128)S(1)}, f32[2,4,32,8,128]{4,3,2,1,0:T(8,128)S(1)}, f32[4,32,8,128]{3,2,1,0:T(8,128)S(1)}) custom-call(f32[4,32,8,128]{3,2,1,0:T(8,128)S(1)} %bitcast.22, f32[2,4,32,8,128]{4,3,2,1,0:T(8,128)S(1)} %bitcast.18, f32[4,32,8,128]{3,2,1,0:T(8,128)S(1)} %bitcast.23), custom_call_target="tpu_custom_call" | custom-call | tf_op jit(solution)/shard_map/pallas_call | solution.py:317
  55.8 0.8 %copy.9 = f32[4,8,4096]{2,1,0:T(8,128)} copy(f32[4,8,4096]{2,1,0:T(8,128)S(1)} %bitcast.21) | data formatting | bytes 1048576
  56.6 1.0 %copy.10 = f32[2,4,8,4096]{3,2,1,0:T(8,128)} copy(f32[2,4,8,4096]{3,2,1,0:T(8,128)S(1)} %bitcast.19) | data formatting | bytes 2097152
  57.6 0.8 %copy.11 = f32[4,8,4096]{2,1,0:T(8,128)} copy(f32[4,8,4096]{2,1,0:T(8,128)S(1)} %bitcast.20) | data formatting | bytes 1048576
Async XLA Ops:
  0.6 1.2 %copy-start = (f32[2,4,8,4096]{3,2,1,0:T(8,128)S(1)}, f32[2,4,8,4096]{3,2,1,0:T(8,128)}, u32[]{:S(2)}) copy-start(f32[2,4,8,4096]{3,2,1,0:T(8,128)} %param.4) | copy-start | bytes 3145732
  1.9 1.0 %copy-start.1 = (f32[4,8,4096]{2,1,0:T(8,128)S(1)}, f32[4,8,4096]{2,1,0:T(8,128)}, u32[]{:S(2)}) copy-start(f32[4,8,4096]{2,1,0:T(8,128)} %param.3) | copy-start | bytes 1572868
  2.9 1.0 %copy-start.2 = (f32[4,8,4096]{2,1,0:T(8,128)S(1)}, f32[4,8,4096]{2,1,0:T(8,128)}, u32[]{:S(2)}) copy-start(f32[4,8,4096]{2,1,0:T(8,128)} %param.5) | copy-start | bytes 1572868
where the time goes:
time: 59.1 us; the launch traced here: 58.3 us
  Pallas kernels  51.8 us (88%)
  local copies, waits for them, and re-layouts  5.86 us (10%)
  between operations  0.65 us (1%)
    pallas_call x1, Pallas kernels, on_device(): pl.pallas_call(kernel, out_shape=(jax.ShapeDtypeStruct(shape, f32), jax.S...  51.8 us
    unnamed x9, local copies, waits for them, and re-layouts  5.86 us

commit v1 on v0

v1 whole, which is shorter than its diff:
```python
import jax
import jax.numpy as jnp
from jax import lax
from jax.experimental import pallas as pl
from jax.experimental.pallas import tpu as pltpu
from jax.sharding import PartitionSpec as P

MESH = pl.DeviceIdType.MESH
NEWTON = 4
LANES = 128
ROWS = 8
QUARTER = 8
HALO = 3
LINE = 32
PIECES = LANES // LINE
SIDES = 2
FACES = 11


def inverse(value):
    return pl.reciprocal(value, approx=False)


def edges(values):
    d = values[1:] - values[:-1]
    here = d[1:-1]
    size = jnp.abs(here)
    sign = jnp.where(here >= 0.0, 1.0, -1.0)
    raw = 0.5 * size + sign * ((d[:-2] - d[2:]) * (1.0 / 12.0))
    to_face = jnp.minimum(jnp.maximum(raw, 0.0), size)
    beyond = size - to_face
    cells = values[2:-2]
    left = cells + sign[1:] * jnp.minimum(to_face[1:], 2.0 * beyond[:-1])
    right = cells - sign[:-1] * jnp.minimum(beyond[:-1], 2.0 * to_face[1:])
    return left[:-1], right[1:]


def fluxes(left, right, ratio):
    rho_l, un_l, ut_l, p_l = left
    rho_r, un_r, ut_r, p_r = right
    a_l = 1.2 * rho_l
    a_r = 1.2 * rho_r
    cc_l = (1.4 * rho_l) * p_l
    cc_r = (1.4 * rho_r) * p_r
    h_l = 0.5 * cc_l
    h_r = 0.5 * cc_r
    du = un_l - un_r
    dp = p_l - p_r
    inv_l = lax.rsqrt(cc_l)
    inv_r = lax.rsqrt(cc_r)
    e_r = cc_r + a_r * dp
    floor_y = 0.1 * jnp.minimum(p_l, p_r) - p_l
    y = (du - dp * inv_r) * inverse(inv_l + inv_r)
    y = jnp.maximum(y, floor_y)
    for _ in range(NEWTON):
        s_l = lax.rsqrt(a_l * y + cc_l)
        s_r = lax.rsqrt(a_r * y + e_r)
        slope = s_l * (0.5 + h_l * (s_l * s_l)) + s_r * (0.5 + h_r * (s_r * s_r))
        gap = y * s_l + ((y + dp) * s_r - du)
        y = jnp.maximum(y - gap * inverse(slope), floor_y)
    s_l = lax.rsqrt(a_l * y + cc_l)
    s_r = lax.rsqrt(a_r * y + e_r)
    pstar = y + p_l
    ustar = 0.5 * ((un_l + un_r) + ((y + dp) * s_r - y * s_l))
    from_left = ustar >= 0.0
    rho = jnp.where(from_left, rho_l, rho_r)
    un = jnp.where(from_left, un_l, un_r)
    ut = jnp.where(from_left, ut_l, ut_r)
    p = jnp.where(from_left, p_l, p_r)
    u_r = ratio * ustar
    mass = u_r * rho
    normal = mass * ustar + ratio * pstar
    trans = mass * ut
    energy = u_r * (2.5 * p + pstar) + (0.5 * mass) * (un * un + ut * ut)
    return mass, normal, trans, energy


def updated(cells, change):
    rho, un, ut, p = cells
    mass, normal, trans, lost = change
    mn = rho * un
    mt = rho * ut
    energy = 2.5 * p + 0.5 * (mn * un + mt * ut)
    rho = rho - mass
    mn = mn - normal
    mt = mt - trans
    energy = energy - lost
    inv = inverse(rho)
    un = mn * inv
    ut = mt * inv
    return rho, un, ut, 0.4 * energy - 0.2 * (mn * un + mt * ut)


def turn_in(source, turned):
    for f in range(4):
        for side in range(SIDES):
            across = source(f, side).T
            for piece in range(PIECES):
                for k in range(LINE // ROWS):
                    at = piece * LINE + k * ROWS
                    turned[f, pl.ds((HALO + k * ROWS) * ROWS + side * PIECES + piece, ROWS, stride=ROWS)] = across[at : at + ROWS]
    shape = (ROWS, LANES)
    row = lax.broadcasted_iota(jnp.int32, shape, 0)
    piece = row & (PIECES - 1)
    lane = lax.broadcasted_iota(jnp.int32, shape, 1)
    for f in range(4):
        for k in range(HALO):
            v = turned[f, pl.ds((LINE + k) * ROWS, ROWS)]
            w = pltpu.roll(v, ROWS, 1)
            seam = jnp.where(lane < ROWS, pltpu.roll(w, 1, 0), pltpu.roll(w, 5, 0))
            turned[f, pl.ds(k * ROWS, ROWS)] = jnp.where(piece == 0, seam, pltpu.roll(v, 1, 0))
            v = turned[f, pl.ds((HALO + k) * ROWS, ROWS)]
            w = pltpu.roll(v, LANES - ROWS, 1)
            seam = jnp.where(lane >= LANES - ROWS, pltpu.roll(w, 7, 0), pltpu.roll(w, 3, 0))
            turned[f, pl.ds((HALO + LINE + k) * ROWS, ROWS)] = jnp.where(piece == PIECES - 1, seam, pltpu.roll(v, 7, 0))


def turn_out(turned, target):
    for f in range(4):
        for side in range(SIDES):
            parts = [
                turned[f, pl.ds((1 + k * ROWS) * ROWS + side * PIECES + piece, ROWS, stride=ROWS)]
                for piece in range(PIECES)
                for k in range(LINE // ROWS)
            ]
            target(f, side, jnp.concatenate(parts, axis=0).T)


def column_sweep(source, target, turned, swept, ratio):
    turn_in(source, turned)

    def some(part, last):
        at = pl.multiple_of(part * (FACES * ROWS), ROWS)
        cells = [
            turned[f, pl.ds(at, (FACES + 5) * ROWS)].reshape(FACES + 5, ROWS, LANES) for f in range(4)
        ]
        sides = [edges(c) for c in cells]
        flux = fluxes([s[0] for s in sides], [s[1] for s in sides], ratio)
        change = [now - jnp.concatenate([old, now[:-1]], axis=0) for now, old in zip(flux, last)]
        for f, value in enumerate(updated([c[2:-3] for c in cells], change)):
            swept[f, pl.ds(at, FACES * ROWS)] = value.reshape(FACES * ROWS, LANES)
        return tuple(now[-1:] for now in flux)

    none = jnp.zeros((1, ROWS, LANES), jnp.float32)
    lax.fori_loop(0, (LINE + 1) // FACES, some, (none,) * 4)
    turn_out(swept, target)


def kernel(
    density, velocity, pressure, new_density, new_velocity, new_pressure,
    start, first, second, final, turned, swept, to_up, to_down, from_up, from_down,
    in_sem, out_sem, send_sem, recv_sem, ready_sem,
):
    slab = lax.axis_index("slab")
    me = lax.axis_index("pencil")
    count = lax.axis_size("pencil")
    up = lax.rem(me + 1, count)
    down = lax.rem(me + count - 1, count)
    planes = start.shape[1]
    quarters = start.shape[2] // (QUARTER * ROWS)
    units = planes * quarters

    barrier = pltpu.get_barrier_semaphore()
    pl.semaphore_signal(barrier, inc=1, device_id=(slab, down), device_id_type=MESH)

    def load(plane, f):
        source = (density.at[plane], velocity.at[0, plane], velocity.at[1, plane], pressure.at[plane])[f]
        return pltpu.make_async_copy(source, start.at[f, plane], in_sem.at[f, plane])

    for plane in range(planes):
        for f in range(4):
            load(plane, f).start()

    def half(ref, plane):
        return lambda f, side: ref[f, plane, pl.ds(side * LANES, LANES)]

    def into(ref, plane):
        def put(f, side, value):
            ref[f, plane, pl.ds(side * LANES, LANES)] = value

        return put

    def copy_up(unit):
        return pltpu.make_async_remote_copy(
            to_up.at[unit], from_down.at[unit], send_sem.at[0, unit], recv_sem.at[0, unit],
            device_id=(slab, up), device_id_type=MESH,
        )

    def copy_down(unit):
        return pltpu.make_async_remote_copy(
            to_down.at[unit], from_up.at[unit], send_sem.at[1, unit], recv_sem.at[1, unit],
            device_id=(slab, down), device_id_type=MESH,
        )

    def line(quarter, row):
        return pl.ds(quarter * (QUARTER * ROWS) + row, QUARTER, stride=ROWS)

    def first_sweep(plane, carry):
        for f in range(4):
            load(plane, f).wait()
        column_sweep(half(start, plane), into(first, plane), turned, swept, 0.025)
        for quarter in range(quarters):
            unit = plane * quarters + quarter
            for f in range(4):
                for row in range(HALO):
                    to_up[unit, f * HALO + row] = first[f, plane, line(quarter, ROWS - HALO + row)]
                    to_down[unit, f * HALO + row] = first[f, plane, line(quarter, row)]

        @pl.when(plane == 0)
        def _():
            pl.semaphore_wait(barrier, 1)
            pl.semaphore_signal(ready_sem, inc=1, device_id=(slab, up), device_id_type=MESH)

        for quarter in range(quarters):
            copy_up(plane * quarters + quarter).start()
        return carry

    lax.fori_loop(0, planes, first_sweep, 0)
    pl.semaphore_wait(ready_sem, 1)

    def send_down(unit, carry):
        copy_down(unit).start()
        return carry

    lax.fori_loop(0, units, send_down, 0)

    def row_sweep(unit):
        plane, quarter = unit // quarters, lax.rem(unit, quarters)
        copy_up(unit).wait_recv()
        copy_down(unit).wait_recv()
        sides, cells = [], []
        for f in (0, 2, 1, 3):
            own = [first[f, plane, line(quarter, row)][None] for row in range(ROWS)]
            below = from_down[unit, pl.ds(f * HALO, HALO)]
            above = from_up[unit, pl.ds(f * HALO, HALO)]
            sides.append(edges(jnp.concatenate([below, *own, above], axis=0)))
            cells.append(jnp.concatenate(own, axis=0))
        flux = fluxes([s[0] for s in sides], [s[1] for s in sides], 0.05)
        new = updated(cells, [now[1:] - now[:-1] for now in flux])
        for f, value in zip((0, 2, 1, 3), new):
            for row in range(ROWS):
                second[f, plane, line(quarter, row)] = value[row]

    def store(plane, f):
        target = (
            new_density.at[plane], new_velocity.at[0, plane], new_velocity.at[1, plane], new_pressure.at[plane],
        )[f]
        return pltpu.make_async_copy(final.at[f, plane], target, out_sem.at[f, plane])

    def later(plane, carry):
        def row_sweeps(quarter, inner):
            row_sweep(plane * quarters + quarter)
            return inner

        lax.fori_loop(0, quarters, row_sweeps, 0)
        column_sweep(half(second, plane), into(final, plane), turned, swept, 0.025)
        for f in range(4):
            store(plane, f).start()
        return carry

    lax.fori_loop(0, planes, later, 0)

    def sent(unit, carry):
        copy_up(unit).wait_send()
        copy_down(unit).wait_send()
        return carry

    lax.fori_loop(0, units, sent, 0)
    for plane in range(planes):
        for f in range(4):
            store(plane, f).wait()


def on_device(density, velocity, pressure):
    planes, rows, columns = density.shape
    blocks = columns // LANES
    units = planes * blocks // QUARTER

    def blocked(a):
        lead = a.shape[:-2]
        return jnp.swapaxes(a.reshape(*lead, rows, blocks, LANES), -3, -2).reshape(*lead, blocks * rows, LANES)

    def unblocked(a):
        lead = a.shape[:-2]
        return jnp.swapaxes(a.reshape(*lead, blocks, rows, LANES), -3, -2).reshape(*lead, rows, columns)

    hbm = pl.BlockSpec(memory_space=pltpu.HBM)
    shape = (planes, blocks * rows, LANES)
    f32 = jnp.float32
    halo = (units, 4 * HALO, QUARTER, LANES)
    outs = pl.pallas_call(
        kernel,
        out_shape=(
            jax.ShapeDtypeStruct(shape, f32),
            jax.ShapeDtypeStruct((2, *shape), f32),
            jax.ShapeDtypeStruct(shape, f32),
        ),
        in_specs=[hbm] * 3,
        out_specs=(hbm,) * 3,
        scratch_shapes=[
            pltpu.VMEM((4, *shape), f32),
            pltpu.VMEM((4, *shape), f32),
            pltpu.VMEM((4, *shape), f32),
            pltpu.VMEM((4, *shape), f32),
            pltpu.VMEM((4, (LINE + 2 * HALO) * ROWS, LANES), f32),
            pltpu.VMEM((4, (LINE + 1) * ROWS, LANES), f32),
            pltpu.VMEM(halo, f32),
            pltpu.VMEM(halo, f32),
            pltpu.VMEM(halo, f32),
            pltpu.VMEM(halo, f32),
            pltpu.SemaphoreType.DMA((4, planes)),
            pltpu.SemaphoreType.DMA((4, planes)),
            pltpu.SemaphoreType.DMA((2, units)),
            pltpu.SemaphoreType.DMA((2, units)),
            pltpu.SemaphoreType.REGULAR,
        ],
        compiler_params=pltpu.CompilerParams(
            collective_id=0, has_side_effects=True, vmem_limit_bytes=48 * 2**20
        ),
    )(*(pltpu.with_memory_space_constraint(blocked(a), pltpu.HBM) for a in (density, velocity, pressure)))
    return tuple(unblocked(a) for a in outs)


def solution(mesh):
    one = P("slab", "pencil", None)
    two = P(None, "slab", "pencil", None)
    return jax.shard_map(on_device, mesh=mesh, in_specs=(one, two, one), out_specs=(one, two, one), check_vma=False)
```

time: 59.1 us -> 50.2 us (0.85)
  Pallas kernels: 51.8 us -> 46.7 us
  local copies, waits for them, and re-layouts: 5.86 us -> 2.56 us
    pallas_call x1, Pallas kernels: 51.8 us -> 46.7 us  [on_device(): pl.pallas_call(kernel, out_shape=(jax.ShapeDtypeStruct(shape, f32), jax.S...]
    unnamed x9 -> x3, local copies, waits for them, and re-layouts: 5.86 us -> 2.56 us
where the time goes in v1:
time: 50.2 us; the launch traced here: 49.9 us
  Pallas kernels  46.7 us (93%)
  local copies, waits for them, and re-layouts  2.56 us (5%)
  between operations  0.64 us (1%)
    pallas_call x1, Pallas kernels, on_device(): pl.pallas_call(kernel, out_shape=(jax.ShapeDtypeStruct(shape, f32), jax.S...  46.7 us
    unnamed x3, local copies, waits for them, and re-layouts  2.56 us

profile of v1, /device:TPU:96, one launch (start us, length us, event | category | flops | bytes accessed | tf_op | source)
XLA Modules:
  0.0 49.9 jit_solution(7302614954878589702)
XLA Ops:
  0.6 46.7 %shard_map.58 = (f32[4,256,128]{2,1,0:T(8,128)S(1)}, f32[2,4,256,128]{3,2,1,0:T(8,128)S(1)}, f32[4,256,128]{2,1,0:T(8,128)S(1)}) custom-call(f32[4,256,128]{2,1,0:T(8,128)} %bitcast.34, f32[2,4,256,128]{3,2,1,0:T(8,128)} %bitcast.33, f32[4,256,128]{2,1,0:T(8,128)} %bitcast.35), custom_call_target="tpu_custom_call" | custom-call | tf_op jit(solution)/shard_map/pallas_call | solution.py:291
  47.3 0.8 %copy.9 = f32[4,8,4096]{2,1,0:T(8,128)} copy(f32[4,8,4096]{2,1,0:T(8,128)S(1)} %bitcast.32) | data formatting | bytes 1048576
  48.1 1.0 %copy.10 = f32[2,4,8,4096]{3,2,1,0:T(8,128)} copy(f32[2,4,8,4096]{3,2,1,0:T(8,128)S(1)} %bitcast.30) | data formatting | bytes 2097152
  49.1 0.8 %copy.11 = f32[4,8,4096]{2,1,0:T(8,128)} copy(f32[4,8,4096]{2,1,0:T(8,128)S(1)} %bitcast.31) | data formatting | bytes 1048576

commit v2 on v1

--- a/solution.py
+++ b/solution.py
@@ -146,10 +146,25 @@
     turn_out(swept, target)
 
 
+def half(ref, *index):
+    return lambda f, side: ref[(f, *index, pl.ds(side * LANES, LANES))]
+
+
+def into(ref, *index):
+    def put(f, side, value):
+        ref[(f, *index, pl.ds(side * LANES, LANES))] = value
+
+    return put
+
+
+def line(quarter, row):
+    return pl.ds(quarter * (QUARTER * ROWS) + row, QUARTER, stride=ROWS)
+
+
 def kernel(
-    density, velocity, pressure, new_density, new_velocity, new_pressure,
-    start, first, second, final, turned, swept, to_up, to_down, from_up, from_down,
-    in_sem, out_sem, send_sem, recv_sem, ready_sem,
+    density, velocity, pressure, done, left,
+    start, first, outer, turned, swept, to_up, to_down, from_up, from_down,
+    in_sem, send_sem, recv_sem, ready_sem,
 ):
     slab = lax.axis_index("slab")
     me = lax.axis_index("pencil")
@@ -158,7 +173,6 @@
     down = lax.rem(me + count - 1, count)
     planes = start.shape[1]
     quarters = start.shape[2] // (QUARTER * ROWS)
-    units = planes * quarters
 
     barrier = pltpu.get_barrier_semaphore()
     pl.semaphore_signal(barrier, inc=1, device_id=(slab, down), device_id_type=MESH)
@@ -170,15 +184,6 @@
     for plane in range(planes):
         for f in range(4):
             load(plane, f).start()
-
-    def half(ref, plane):
-        return lambda f, side: ref[f, plane, pl.ds(side * LANES, LANES)]
-
-    def into(ref, plane):
-        def put(f, side, value):
-            ref[f, plane, pl.ds(side * LANES, LANES)] = value
-
-        return put
 
     def copy_up(unit):
         return pltpu.make_async_remote_copy(
@@ -192,42 +197,81 @@
             device_id=(slab, down), device_id_type=MESH,
         )
 
-    def line(quarter, row):
-        return pl.ds(quarter * (QUARTER * ROWS) + row, QUARTER, stride=ROWS)
-
-    def first_sweep(plane, carry):
-        for f in range(4):
-            load(plane, f).wait()
-        column_sweep(half(start, plane), into(first, plane), turned, swept, 0.025)
+    def pack(ref, plane):
         for quarter in range(quarters):
             unit = plane * quarters + quarter
             for f in range(4):
                 for row in range(HALO):
-                    to_up[unit, f * HALO + row] = first[f, plane, line(quarter, ROWS - HALO + row)]
-                    to_down[unit, f * HALO + row] = first[f, plane, line(quarter, row)]
-
-        @pl.when(plane == 0)
-        def _():
-            pl.semaphore_wait(barrier, 1)
-            pl.semaphore_signal(ready_sem, inc=1, device_id=(slab, up), device_id_type=MESH)
-
+                    to_up[unit, f * HALO + row] = ref[f, plane, line(quarter, ROWS - HALO + row)]
+                    to_down[unit, f * HALO + row] = ref[f, plane, line(quarter, row)]
+
+    def send(copy, plane):
         for quarter in range(quarters):
-            copy_up(plane * quarters + quarter).start()
+            copy(plane * quarters + quarter).start()
+
+    for f in range(4):
+        load(0, f).wait()
+    pack(start, 0)
+    pl.semaphore_wait(barrier, 1)
+    pl.semaphore_signal(ready_sem, inc=1, device_id=(slab, up), device_id_type=MESH)
+    send(copy_up, 0)
+
+    def first_sweep(plane, carry):
+        @pl.when(plane > 0)
+        def _():
+            for f in range(4):
+                load(plane, f).wait()
+
+        column_sweep(half(start, plane), into(first, plane), turned, swept, 0.025)
+
+        @pl.when(plane > 0)
+        def _():
+            pack(first, plane)
+            send(copy_up, plane)
+
+        @pl.when(plane == 1)
+        def _():
+            pl.semaphore_wait(ready_sem, 1)
+
+        @pl.when(plane > 0)
+        def _():
+            send(copy_down, plane - 1)
+
+        @pl.when(plane == planes - 1)
+        def _():
+            send(copy_down, plane)
+
         return carry
 
     lax.fori_loop(0, planes, first_sweep, 0)
-    pl.semaphore_wait(ready_sem, 1)
-
-    def send_down(unit, carry):
-        copy_down(unit).start()
-        return carry
-
-    lax.fori_loop(0, units, send_down, 0)
-
-    def row_sweep(unit):
-        plane, quarter = unit // quarters, lax.rem(unit, quarters)
+
+    def arrive(unit):
         copy_up(unit).wait_recv()
         copy_down(unit).wait_recv()
+
+    def outer_sweep():
+        for quarter in range(quarters):
+            arrive(quarter)
+            for f in range(4):
+                for row in range(HALO):
+                    outer[f, line(quarter, row)] = from_down[quarter, f * HALO + row]
+                    outer[f, line(quarter, HALO + row)] = from_up[quarter, f * HALO + row]
+                for row in range(2 * HALO, ROWS):
+                    outer[f, line(quarter, row)] = from_down[quarter, f * HALO]
+        column_sweep(half(outer), into(outer), turned, swept, 0.025)
+        for quarter in range(quarters):
+            for f in range(4):
+                for row in range(HALO):
+                    from_down[quarter, f * HALO + row] = outer[f, line(quarter, row)]
+                    from_up[quarter, f * HALO + row] = outer[f, line(quarter, HALO + row)]
+
+    def row_sweep(plane, quarter):
+        unit = plane * quarters + quarter
+
+        @pl.when(plane > 0)
+        def _():
+            arrive(unit)
+
         sides, cells = [], []
         for f in (0, 2, 1, 3):
             own = [first[f, plane, line(quarter, row)][None] for row in range(ROWS)]
@@ -239,34 +283,49 @@
         new = updated(cells, [now[1:] - now[:-1] for now in flux])
         for f, value in zip((0, 2, 1, 3), new):
             for row in range(ROWS):
-                second[f, plane, line(quarter, row)] = value[row]
+                left[f, line(quarter, row)] = value[row]
+
+    def later(plane, carry):
+        pl.when(plane == 0)(outer_sweep)
+
+        def row_sweeps(quarter, inner):
+            row_sweep(plane, quarter)
+            return inner
+
+        lax.fori_loop(0, quarters, row_sweeps, 0)
+
+        @pl.when(plane < planes - 1)
+        def _():
+            column_sweep(half(left), into(done, plane), turned, swept, 0.025)
+
+        return carry
+
+    lax.fori_loop(0, planes, later, 0)
+    def sent(unit, carry):
+        copy_up(unit).wait_send()
+        copy_down(unit).wait_send()
+        return carry
+
+    lax.fori_loop(0, planes * quarters, sent, 0)
+
+
+def last_kernel(done, left, new_density, new_velocity, new_pressure, final, turned, swept, out_sem):
+    before = done.shape[1]
 
     def store(plane, f):
         target = (
             new_density.at[plane], new_velocity.at[0, plane], new_velocity.at[1, plane], new_pressure.at[plane],
         )[f]
-        return pltpu.make_async_copy(final.at[f, plane], target, out_sem.at[f, plane])
-
-    def later(plane, carry):
-        def row_sweeps(quarter, inner):
-            row_sweep(plane * quarters + quarter)
-            return inner
-
-        lax.fori_loop(0, quarters, row_sweeps, 0)
-        column_sweep(half(second, plane), into(final, plane), turned, swept, 0.025)
+        source = final.at[f] if plane == before else done.at[f, plane]
+        return pltpu.make_async_copy(source, target, out_sem.at[f, plane])
+
+    for plane in range(before):
         for f in range(4):
             store(plane, f).start()
-        return carry
-
-    lax.fori_loop(0, planes, later, 0)
-
-    def sent(unit, carry):
-        copy_up(unit).wait_send()
-        copy_down(unit).wait_send()
-        return carry
-
-    lax.fori_loop(0, units, sent, 0)
-    for plane in range(planes):
+    column_sweep(half(left), into(final), turned, swept, 0.025)
+    for f in range(4):
+        store(before, f).start()
+    for plane in range(before + 1):
         for f in range(4):
             store(plane, f).wait()
 
@@ -278,46 +337,53 @@
 
     def blocked(a):
         lead = a.shape[:-2]
-        return jnp.swapaxes(a.reshape(*lead, rows, blocks, LANES), -3, -2).reshape(*lead, blocks * rows, LANES)
+        a = jnp.swapaxes(a.reshape(*lead, rows, blocks, LANES), -3, -2).reshape(*lead, blocks * rows, LANES)
+        return pltpu.with_memory_space_constraint(a, pltpu.HBM)
 
     def unblocked(a):
         lead = a.shape[:-2]
         return jnp.swapaxes(a.reshape(*lead, blocks, rows, LANES), -3, -2).reshape(*lead, rows, columns)
 
     hbm = pl.BlockSpec(memory_space=pltpu.HBM)
-    shape = (planes, blocks * rows, LANES)
+    vmem = pl.BlockSpec(memory_space=pltpu.VMEM)
+    plane = (blocks * rows, LANES)
     f32 = jnp.float32
     halo = (units, 4 * HALO, QUARTER, LANES)
-    outs = pl.pallas_call(
+    work = [
+        pltpu.VMEM((4, (LINE + 2 * HALO) * ROWS, LANES), f32),
+        pltpu.VMEM((4, (LINE + 1) * ROWS, LANES), f32),
+    ]
+    done, left = pl.pallas_call(
         kernel,
-        out_shape=(
-            jax.ShapeDtypeStruct(shape, f32),
-            jax.ShapeDtypeStruct((2, *shape), f32),
-            jax.ShapeDtypeStruct(shape, f32),
-        ),
+        out_shape=(pltpu.VMEM((4, planes - 1, *plane), f32), pltpu.VMEM((4, *plane), f32)),
         in_specs=[hbm] * 3,
-        out_specs=(hbm,) * 3,
+        out_specs=(vmem, vmem),
         scratch_shapes=[
-            pltpu.VMEM((4, *shape), f32),
-            pltpu.VMEM((4, *shape), f32),
-            pltpu.VMEM((4, *shape), f32),
-            pltpu.VMEM((4, *shape), f32),
-            pltpu.VMEM((4, (LINE + 2 * HALO) * ROWS, LANES), f32),
-            pltpu.VMEM((4, (LINE + 1) * ROWS, LANES), f32),
+            pltpu.VMEM((4, planes, *plane), f32),
+            pltpu.VMEM((4, planes, *plane), f32),
+            pltpu.VMEM((4, *plane), f32),
+            *work,
             pltpu.VMEM(halo, f32),
             pltpu.VMEM(halo, f32),
             pltpu.VMEM(halo, f32),
             pltpu.VMEM(halo, f32),
-            pltpu.SemaphoreType.DMA((4, planes)),
             pltpu.SemaphoreType.DMA((4, planes)),
             pltpu.SemaphoreType.DMA((2, units)),
             pltpu.SemaphoreType.DMA((2, units)),
             pltpu.SemaphoreType.REGULAR,
         ],
         compiler_params=pltpu.CompilerParams(
-            collective_id=0, has_side_effects=True, vmem_limit_bytes=48 * 2**20
+            collective_id=0, has_side_effects=True, vmem_limit_bytes=32 * 2**20
         ),
-    )(*(pltpu.with_memory_space_constraint(blocked(a), pltpu.HBM) for a in (density, velocity, pressure)))
+    )(blocked(density), blocked(velocity), blocked(pressure))
+    outs = pl.pallas_call(
+        last_kernel,
+        out_shape=(pltpu.HBM((planes, *plane), f32), pltpu.HBM((2, planes, *plane), f32), pltpu.HBM((planes, *plane), f32)),
+        in_specs=[vmem] * 2,
+        out_specs=(hbm,) * 3,
+        scratch_shapes=[pltpu.VMEM((4, *plane), f32), *work, pltpu.SemaphoreType.DMA((4, planes))],
+        compiler_params=pltpu.CompilerParams(vmem_limit_bytes=16 * 2**20),
+    )(*(pltpu.with_memory_space_constraint(a, pltpu.VMEM) for a in (done, left)))
     return tuple(unblocked(a) for a in outs)
 
 

time: 50.2 us -> 46.1 us (0.918)
  local copies, waits for them, and re-layouts: 2.56 us -> 0 us
  Pallas kernels: 46.7 us -> 45.2 us
    unnamed x3 -> x0, local copies, waits for them, and re-layouts: 2.56 us -> none
    pallas_call x1 -> x2, Pallas kernels: 46.7 us -> 45.2 us  [the longest x1 42.5 us: on_device(): pl.pallas_call(kernel, out_shape=(pltpu.VMEM((4, planes - 1, *plane), f32...]
where the time goes in v2:
time: 46.1 us; the launch traced here: 45.9 us
  Pallas kernels  45.2 us (98%)
  between operations  0.64 us (1%)
    pallas_call x1, Pallas kernels, on_device(): pl.pallas_call(kernel, out_shape=(pltpu.VMEM((4, planes - 1, *plane), f32...  42.5 us
    pallas_call x1, Pallas kernels, on_device(): pl.pallas_call(last_kernel, out_shape=(pltpu.HBM((planes, *plane), f32),...  2.74 us

profile of v2, /device:TPU:96, one launch (start us, length us, event | category | flops | bytes accessed | tf_op | source)
XLA Modules:
  0.0 45.9 jit_solution(2752605019762620369)
XLA Ops:
  0.6 42.5 %shard_map.58 = (f32[4,3,256,128]{3,2,1,0:T(8,128)S(1)}, f32[4,256,128]{2,1,0:T(8,128)S(1)}) custom-call(f32[4,256,128]{2,1,0:T(8,128)} %bitcast.31, f32[2,4,256,128]{3,2,1,0:T(8,128)} %bitcast.30, f32[4,256,128]{2,1,0:T(8,128)} %bitcast.32), custom_call_target="tpu_custom_call" | custom-call | tf_op jit(solution)/shard_map/pallas_call | solution.py:356
  43.1 2.7 %shard_map.59 = (f32[4,256,128]{2,1,0:T(8,128)}, f32[2,4,256,128]{3,2,1,0:T(8,128)}, f32[4,256,128]{2,1,0:T(8,128)}) custom-call(f32[4,3,256,128]{3,2,1,0:T(8,128)S(1)} %get-tuple-element.8.done, f32[4,256,128]{2,1,0:T(8,128)S(1)} %get-tuple-element.9.left), custom_call_target="tpu_custom_call" | custom-call | tf_op jit(solution)/shard_map/pallas_call | solution.py:379

commit v3 on v2

--- a/solution.py
+++ b/solution.py
@@ -11,6 +11,7 @@
 ROWS = 8
 QUARTER = 8
 HALO = 3
+GROUP = 8
 LINE = 32
 PIECES = LANES // LINE
 SIDES = 2
@@ -174,8 +175,13 @@
     planes = start.shape[1]
     quarters = start.shape[2] // (QUARTER * ROWS)
 
+    place = lax.rem(me, GROUP)
     barrier = pltpu.get_barrier_semaphore()
     pl.semaphore_signal(barrier, inc=1, device_id=(slab, down), device_id_type=MESH)
+
+    @pl.when(place < GROUP - 1)
+    def _():
+        pl.semaphore_signal(barrier, inc=1, device_id=(slab, up), device_id_type=MESH)
 
     def load(plane, f):
         source = (density.at[plane], velocity.at[0, plane], velocity.at[1, plane], pressure.at[plane])[f]
@@ -185,17 +191,30 @@
         for f in range(4):
             load(plane, f).start()
 
-    def copy_up(unit):
+    def copy_up(unit, n):
+        part = pl.ds(unit, n)
         return pltpu.make_async_remote_copy(
-            to_up.at[unit], from_down.at[unit], send_sem.at[0, unit], recv_sem.at[0, unit],
+            to_up.at[part], from_down.at[part], send_sem.at[0, unit], recv_sem.at[0, unit],
             device_id=(slab, up), device_id_type=MESH,
         )
 
-    def copy_down(unit):
+    def copy_down(unit, n):
+        part = pl.ds(unit, n)
         return pltpu.make_async_remote_copy(
-            to_down.at[unit], from_up.at[unit], send_sem.at[1, unit], recv_sem.at[1, unit],
+            to_down.at[part], from_up.at[part], send_sem.at[1, unit], recv_sem.at[1, unit],
             device_id=(slab, down), device_id_type=MESH,
         )
+
+    def messages(plane, act):
+        @pl.when(plane < planes - 1)
+        def _():
+            for quarter in range(0, quarters, 2):
+                act(plane * quarters + quarter, 2)
+
+        @pl.when(plane == planes - 1)
+        def _():
+            for quarter in range(quarters):
+                act(plane * quarters + quarter, 1)
 
     def pack(ref, plane):
         for quarter in range(quarters):
@@ -206,17 +225,33 @@
                     to_down[unit, f * HALO + row] = ref[f, plane, line(quarter, row)]
 
     def send(copy, plane):
-        for quarter in range(quarters):
-            copy(plane * quarters + quarter).start()
+        messages(plane, lambda unit, n: copy(unit, n).start())
 
     for f in range(4):
         load(0, f).wait()
     pack(start, 0)
-    pl.semaphore_wait(barrier, 1)
-    pl.semaphore_signal(ready_sem, inc=1, device_id=(slab, up), device_id_type=MESH)
+
+    @pl.when(place == 0)
+    def _():
+        pl.semaphore_wait(barrier, 1)
+
+    @pl.when(place > 0)
+    def _():
+        pl.semaphore_wait(barrier, 2)
+
+    @pl.when(place == GROUP - 1)
+    def _():
+        pl.semaphore_signal(ready_sem, inc=1, device_id=(slab, up), device_id_type=MESH)
+
     send(copy_up, 0)
 
-    def first_sweep(plane, carry):
+    @pl.when(place > 0)
+    def _():
+        send(copy_down, 0)
+
+    def first_sweep(step, carry):
+        plane = jnp.where(step < 2, 1 - step, step)
+
         @pl.when(plane > 0)
         def _():
             for f in range(4):
@@ -229,29 +264,30 @@
             pack(first, plane)
             send(copy_up, plane)
 
-        @pl.when(plane == 1)
+        @pl.when(jnp.logical_and(plane == 0, place == 0))
         def _():
             pl.semaphore_wait(ready_sem, 1)
-
-        @pl.when(plane > 0)
-        def _():
-            send(copy_down, plane - 1)
-
-        @pl.when(plane == planes - 1)
-        def _():
-            send(copy_down, plane)
+            send(copy_down, 0)
+
+        @pl.when(step > 1)
+        def _():
+            send(copy_down, step - 1)
+
+        @pl.when(step == planes - 1)
+        def _():
+            send(copy_down, step)
 
         return carry
 
     lax.fori_loop(0, planes, first_sweep, 0)
 
-    def arrive(unit):
-        copy_up(unit).wait_recv()
-        copy_down(unit).wait_recv()
+    def arrive(unit, n):
+        copy_up(unit, n).wait_recv()
+        copy_down(unit, n).wait_recv()
 
     def outer_sweep():
+        messages(0, arrive)
         for quarter in range(quarters):
-            arrive(quarter)
             for f in range(4):
                 for row in range(HALO):
                     outer[f, line(quarter, row)] = from_down[quarter, f * HALO + row]
@@ -268,9 +304,13 @@
     def row_sweep(plane, quarter):
         unit = plane * quarters + quarter
 
-        @pl.when(plane > 0)
-        def _():
-            arrive(unit)
+        @pl.when(jnp.logical_and(jnp.logical_and(plane > 0, plane < planes - 1), lax.rem(quarter, 2) == 0))
+        def _():
+            arrive(unit, 2)
+
+        @pl.when(plane == planes - 1)
+        def _():
+            arrive(unit, 1)
 
         sides, cells = [], []
         for f in (0, 2, 1, 3):
@@ -301,12 +341,12 @@
         return carry
 
     lax.fori_loop(0, planes, later, 0)
-    def sent(unit, carry):
-        copy_up(unit).wait_send()
-        copy_down(unit).wait_send()
-        return carry
-
-    lax.fori_loop(0, planes * quarters, sent, 0)
+    def sent(unit, n):
+        copy_up(unit, n).wait_send()
+        copy_down(unit, n).wait_send()
+
+    for plane in range(planes):
+        messages(plane, sent)
 
 
 def last_kernel(done, left, new_density, new_velocity, new_pressure, final, turned, swept, out_sem):

time: 46.1 us -> 44.6 us (0.967)
  Pallas kernels: 45.2 us -> 43.9 us
    pallas_call x1, Pallas kernels: 42.5 us -> 41.1 us  [on_device(): pl.pallas_call(kernel, out_shape=(pltpu.VMEM((4, planes - 1, *plane), f32...]
where the time goes in v3:
time: 44.6 us; the launch traced here: 44.5 us
  Pallas kernels  43.9 us (98%)
  between operations  0.64 us (1%)
    pallas_call x1, Pallas kernels, on_device(): pl.pallas_call(kernel, out_shape=(pltpu.VMEM((4, planes - 1, *plane), f32...  41.1 us
    pallas_call x1, Pallas kernels, on_device(): pl.pallas_call(last_kernel, out_shape=(pltpu.HBM((planes, *plane), f32),...  2.74 us

profile of v3, /device:TPU:96, one launch (start us, length us, event | category | flops | bytes accessed | tf_op | source)
XLA Modules:
  0.0 44.5 jit_solution(17684913429598907508)
XLA Ops:
  0.6 41.1 %shard_map.58 = (f32[4,3,256,128]{3,2,1,0:T(8,128)S(1)}, f32[4,256,128]{2,1,0:T(8,128)S(1)}) custom-call(f32[4,256,128]{2,1,0:T(8,128)} %bitcast.31, f32[2,4,256,128]{3,2,1,0:T(8,128)} %bitcast.30, f32[4,256,128]{2,1,0:T(8,128)} %bitcast.32), custom_call_target="tpu_custom_call" | custom-call | tf_op jit(solution)/shard_map/pallas_call | solution.py:396
  41.8 2.7 %shard_map.59 = (f32[4,256,128]{2,1,0:T(8,128)}, f32[2,4,256,128]{3,2,1,0:T(8,128)}, f32[4,256,128]{2,1,0:T(8,128)}) custom-call(f32[4,3,256,128]{3,2,1,0:T(8,128)S(1)} %get-tuple-element.8.done, f32[4,256,128]{2,1,0:T(8,128)S(1)} %get-tuple-element.9.left), custom_call_target="tpu_custom_call" | custom-call | tf_op jit(solution)/shard_map/pallas_call | solution.py:419

commit v4 on v3

--- a/solution.py
+++ b/solution.py
@@ -15,6 +15,8 @@
 LINE = 32
 PIECES = LANES // LINE
 SIDES = 2
+HALF_LINE = 16
+LEAD = 4
 FACES = 11
 
 
@@ -116,35 +118,80 @@
             turned[f, pl.ds((HALO + LINE + k) * ROWS, ROWS)] = jnp.where(piece == PIECES - 1, seam, pltpu.roll(v, 7, 0))
 
 
-def turn_out(turned, target):
-    for f in range(4):
-        for side in range(SIDES):
-            parts = [
-                turned[f, pl.ds((1 + k * ROWS) * ROWS + side * PIECES + piece, ROWS, stride=ROWS)]
-                for piece in range(PIECES)
-                for k in range(LINE // ROWS)
-            ]
-            target(f, side, jnp.concatenate(parts, axis=0).T)
-
-
-def column_sweep(source, target, turned, swept, ratio):
-    turn_in(source, turned)
-
+def turn_half(source, beyond, turned):
+    edge = jnp.concatenate([rows for f in range(4) for rows in beyond(f)] * 2, axis=0).T
+    row = lax.broadcasted_iota(jnp.int32, (ROWS, LANES), 0)
+    lane = lax.broadcasted_iota(jnp.int32, (ROWS, LANES), 1)
+    pieces = LANES // HALF_LINE
+    for f in range(4):
+        across = source(f).T
+        for piece in range(pieces):
+            for k in range(HALF_LINE // ROWS):
+                at = piece * HALF_LINE + k * ROWS
+                turned[f, pl.ds((HALO + k * ROWS) * ROWS + piece, ROWS, stride=ROWS)] = across[at : at + ROWS]
+        before = pltpu.roll(edge[LANES - ROWS :], (LANES - 2 * ROWS * f) % LANES, 1)
+        before = jnp.where(lane < ROWS, before, pltpu.roll(across[LANES - ROWS :], ROWS, 1))
+        after = pltpu.roll(edge[:ROWS], LANES - 2 * ROWS * (f + 1), 1)
+        after = jnp.where(lane >= LANES - ROWS, after, pltpu.roll(across[:ROWS], LANES - ROWS, 1))
+        for k in range(HALO):
+            v = turned[f, pl.ds((HALF_LINE + k) * ROWS, ROWS)]
+            first = jnp.broadcast_to(before[ROWS - HALO + k : ROWS - HALO + k + 1], (ROWS, LANES))
+            turned[f, pl.ds(k * ROWS, ROWS)] = jnp.where(row == 0, first, pltpu.roll(v, 1, 0))
+            v = turned[f, pl.ds((HALO + k) * ROWS, ROWS)]
+            last = jnp.broadcast_to(after[k : k + 1], (ROWS, LANES))
+            turned[f, pl.ds((HALO + HALF_LINE + k) * ROWS, ROWS)] = jnp.where(row == ROWS - 1, last, pltpu.roll(v, ROWS - 1, 0))
+
+
+def turn_out(turned, f, line_columns, first):
+    parts = [
+        turned[f, pl.ds((1 + k * ROWS) * ROWS + first + piece, ROWS, stride=ROWS)]
+        for piece in range(LANES // line_columns)
+        for k in range(line_columns // ROWS)
+    ]
+    return jnp.concatenate(parts, axis=0).T
+
+
+def turned_sweep(turned, swept, ratio, faces, steps):
     def some(part, last):
-        at = pl.multiple_of(part * (FACES * ROWS), ROWS)
+        at = pl.multiple_of(part * (faces * ROWS), ROWS)
         cells = [
-            turned[f, pl.ds(at, (FACES + 5) * ROWS)].reshape(FACES + 5, ROWS, LANES) for f in range(4)
+            turned[f, pl.ds(at, (faces + 5) * ROWS)].reshape(faces + 5, ROWS, LANES) for f in range(4)
         ]
         sides = [edges(c) for c in cells]
         flux = fluxes([s[0] for s in sides], [s[1] for s in sides], ratio)
         change = [now - jnp.concatenate([old, now[:-1]], axis=0) for now, old in zip(flux, last)]
         for f, value in enumerate(updated([c[2:-3] for c in cells], change)):
-            swept[f, pl.ds(at, FACES * ROWS)] = value.reshape(FACES * ROWS, LANES)
+            swept[f, pl.ds(at, faces * ROWS)] = value.reshape(faces * ROWS, LANES)
         return tuple(now[-1:] for now in flux)
 
-    none = jnp.zeros((1, ROWS, LANES), jnp.float32)
-    lax.fori_loop(0, (LINE + 1) // FACES, some, (none,) * 4)
-    turn_out(swept, target)
+    none = (jnp.zeros((1, ROWS, LANES), jnp.float32),) * 4
+    if steps == 1:
+        some(0, none)
+    else:
+        lax.fori_loop(0, steps, some, none)
+
+
+def column_sweep(source, target, turned, swept, ratio):
+    turn_in(source, turned)
+    turned_sweep(turned, swept, ratio, FACES, (LINE + 1) // FACES)
+    for f in range(4):
+        for side in range(SIDES):
+            target(f, side, turn_out(swept, f, LINE, side * PIECES))
+
+
+def half_sweep(ref, block, put, turned, swept, ratio):
+    def rows(f, first, n):
+        return ref[f, pl.ds(first * ROWS, n * ROWS)]
+
+    blocks = LANES // ROWS
+    turn_half(
+        lambda f: rows(f, block, blocks),
+        lambda f: (rows(f, block - 1, 1), rows(f, block + blocks, 1)),
+        turned,
+    )
+    turned_sweep(turned, swept, ratio, HALF_LINE + 1, 1)
+    for f in range(4):
+        put(f, turn_out(swept, f, HALF_LINE, 0))
 
 
 def half(ref, *index):
@@ -163,8 +210,8 @@
 
 
 def kernel(
-    density, velocity, pressure, done, left,
-    start, first, outer, turned, swept, to_up, to_down, from_up, from_down,
+    density, velocity, pressure, done, done_half, left,
+    start, first, mid, outer, turned, swept, to_up, to_down, from_up, from_down,
     in_sem, send_sem, recv_sem, ready_sem,
 ):
     slab = lax.axis_index("slab")
@@ -187,9 +234,11 @@
         source = (density.at[plane], velocity.at[0, plane], velocity.at[1, plane], pressure.at[plane])[f]
         return pltpu.make_async_copy(source, start.at[f, plane], in_sem.at[f, plane])
 
-    for plane in range(planes):
+    def load_all(plane):
         for f in range(4):
             load(plane, f).start()
+
+    load_all(0)
 
     def copy_up(unit, n):
         part = pl.ds(unit, n)
@@ -205,6 +254,9 @@
             device_id=(slab, down), device_id_type=MESH,
         )
 
+    def last_order(step):
+        return (step + quarters - 1) % quarters
+
     def messages(plane, act):
         @pl.when(plane < planes - 1)
         def _():
@@ -213,8 +265,8 @@
 
         @pl.when(plane == planes - 1)
         def _():
-            for quarter in range(quarters):
-                act(plane * quarters + quarter, 1)
+            for step in range(quarters):
+                act(plane * quarters + last_order(step), 1)
 
     def pack(ref, plane):
         for quarter in range(quarters):
@@ -229,6 +281,7 @@
 
     for f in range(4):
         load(0, f).wait()
+    load_all(1)
     pack(start, 0)
 
     @pl.when(place == 0)
@@ -243,12 +296,21 @@
     def _():
         pl.semaphore_signal(ready_sem, inc=1, device_id=(slab, up), device_id_type=MESH)
 
-    send(copy_up, 0)
-
-    @pl.when(place > 0)
+    ahead = place == GROUP - 1
+
+    @pl.when(ahead)
     def _():
         send(copy_down, 0)
 
+    send(copy_up, 0)
+
+    @pl.when(jnp.logical_and(place > 0, jnp.logical_not(ahead)))
+    def _():
+        send(copy_down, 0)
+
+    for plane in range(2, planes):
+        load_all(plane)
+
     def first_sweep(step, carry):
         plane = jnp.where(step < 2, 1 - step, step)
 
@@ -262,20 +324,34 @@
         @pl.when(plane > 0)
         def _():
             pack(first, plane)
+
+        def both(unit, n):
+            copy_up(unit, n).start()
+            copy_down(unit, n).start()
+
+        held = jnp.logical_and(place == GROUP - 1, plane >= 2)
+
+        @pl.when(jnp.logical_and(jnp.logical_and(plane > 0, place > 0), jnp.logical_not(held)))
+        def _():
+            messages(plane, both)
+
+        @pl.when(held)
+        def _():
+            send(copy_down, plane)
+
+        @pl.when(jnp.logical_and(plane == 1, place == 0))
+        def _():
             send(copy_up, plane)
 
         @pl.when(jnp.logical_and(plane == 0, place == 0))
         def _():
             pl.semaphore_wait(ready_sem, 1)
             send(copy_down, 0)
-
-        @pl.when(step > 1)
-        def _():
-            send(copy_down, step - 1)
-
-        @pl.when(step == planes - 1)
-        def _():
-            send(copy_down, step)
+            send(copy_down, 1)
+
+        @pl.when(jnp.logical_and(plane > 1, place == 0))
+        def _():
+            messages(plane, both)
 
         return carry
 
@@ -301,17 +377,8 @@
                     from_down[quarter, f * HALO + row] = outer[f, line(quarter, row)]
                     from_up[quarter, f * HALO + row] = outer[f, line(quarter, HALO + row)]
 
-    def row_sweep(plane, quarter):
+    def row_sweep(plane, quarter, ref, place):
         unit = plane * quarters + quarter
-
-        @pl.when(jnp.logical_and(jnp.logical_and(plane > 0, plane < planes - 1), lax.rem(quarter, 2) == 0))
-        def _():
-            arrive(unit, 2)
-
-        @pl.when(plane == planes - 1)
-        def _():
-            arrive(unit, 1)
-
         sides, cells = [], []
         for f in (0, 2, 1, 3):
             own = [first[f, plane, line(quarter, row)][None] for row in range(ROWS)]
@@ -323,24 +390,52 @@
         new = updated(cells, [now[1:] - now[:-1] for now in flux])
         for f, value in zip((0, 2, 1, 3), new):
             for row in range(ROWS):
-                left[f, line(quarter, row)] = value[row]
+                ref[f, line(place, row)] = value[row]
 
     def later(plane, carry):
         pl.when(plane == 0)(outer_sweep)
 
         def row_sweeps(quarter, inner):
-            row_sweep(plane, quarter)
+            @pl.when(jnp.logical_and(plane > 0, lax.rem(quarter, 2) == 0))
+            def _():
+                arrive(plane * quarters + quarter, 2)
+
+            row_sweep(plane, quarter, mid, quarter)
             return inner
 
         lax.fori_loop(0, quarters, row_sweeps, 0)
-
-        @pl.when(plane < planes - 1)
-        def _():
-            column_sweep(half(left), into(done, plane), turned, swept, 0.025)
+        column_sweep(half(mid), into(done, plane), turned, swept, 0.025)
+
+        @pl.when(jnp.logical_and(place == GROUP - 1, plane + 2 >= 2))
+        def _():
+            pl.when(plane < planes - 2)(lambda: send(copy_up, plane + 2))
 
         return carry
 
-    lax.fori_loop(0, planes, later, 0)
+    last = planes - 1
+    lax.fori_loop(0, last, later, 0)
+
+    def put(f, value):
+        done_half[f] = value
+
+    def last_rows(step, carry):
+        quarter = last_order(step)
+        arrive(last * quarters + quarter, 1)
+        row_sweep(last, quarter, left, step)
+
+        @pl.when(step == 0)
+        def _():
+            for f in range(4):
+                left[f, pl.ds(quarters * QUARTER * ROWS, QUARTER * ROWS)] = left[f, pl.ds(0, QUARTER * ROWS)]
+
+        @pl.when(step == quarters - 2)
+        def _():
+            half_sweep(left, LEAD, put, turned, swept, 0.025)
+
+        return carry
+
+    lax.fori_loop(0, quarters, last_rows, 0)
+
     def sent(unit, n):
         copy_up(unit, n).wait_send()
         copy_down(unit, n).wait_send()
@@ -349,25 +444,47 @@
         messages(plane, sent)
 
 
-def last_kernel(done, left, new_density, new_velocity, new_pressure, final, turned, swept, out_sem):
-    before = done.shape[1]
+def last_kernel(done, done_half, left, new_density, new_velocity, new_pressure, final, turned, swept, out_sem, half_sem):
+    planes = done.shape[1]
+    total = done.shape[2]
+    size = final.shape[1]
+
+    def target(plane, f, first, n):
+        part = pl.ds(first, n)
+        return (
+            new_density.at[plane, part], new_velocity.at[0, plane, part],
+            new_velocity.at[1, plane, part], new_pressure.at[plane, part],
+        )[f]
 
     def store(plane, f):
-        target = (
-            new_density.at[plane], new_velocity.at[0, plane], new_velocity.at[1, plane], new_pressure.at[plane],
-        )[f]
-        source = final.at[f] if plane == before else done.at[f, plane]
-        return pltpu.make_async_copy(source, target, out_sem.at[f, plane])
-
-    for plane in range(before):
-        for f in range(4):
+        return pltpu.make_async_copy(done.at[f, plane], target(plane, f, 0, total), out_sem.at[f, plane])
+
+    wrap = LEAD * ROWS
+
+    def store_half(f, part):
+        source, first, n = (
+            (done_half.at[f, pl.ds(0, wrap)], total - wrap, wrap),
+            (done_half.at[f, pl.ds(wrap, size - wrap)], 0, size - wrap),
+            (final.at[f], size - wrap, size),
+        )[part]
+        return pltpu.make_async_copy(source, target(planes, f, first, n), half_sem.at[f, part])
+
+    for f in range(4):
+        for plane in range(planes):
             store(plane, f).start()
-    column_sweep(half(left), into(final), turned, swept, 0.025)
-    for f in range(4):
-        store(before, f).start()
-    for plane in range(before + 1):
-        for f in range(4):
+        store_half(f, 0).start()
+        store_half(f, 1).start()
+
+    def put(f, value):
+        final[f] = value
+        store_half(f, 2).start()
+
+    half_sweep(left, LEAD + LANES // ROWS, put, turned, swept, 0.025)
+    for f in range(4):
+        for plane in range(planes):
             store(plane, f).wait()
+        for part in range(3):
+            store_half(f, part).wait()
 
 
 def on_device(density, velocity, pressure):
@@ -389,18 +506,24 @@
     plane = (blocks * rows, LANES)
     f32 = jnp.float32
     halo = (units, 4 * HALO, QUARTER, LANES)
+    half_plane = (4, LANES, LANES)
     work = [
         pltpu.VMEM((4, (LINE + 2 * HALO) * ROWS, LANES), f32),
         pltpu.VMEM((4, (LINE + 1) * ROWS, LANES), f32),
     ]
-    done, left = pl.pallas_call(
+    middle = pl.pallas_call(
         kernel,
-        out_shape=(pltpu.VMEM((4, planes - 1, *plane), f32), pltpu.VMEM((4, *plane), f32)),
+        out_shape=(
+            pltpu.VMEM((4, planes - 1, *plane), f32),
+            pltpu.VMEM(half_plane, f32),
+            pltpu.VMEM((4, (blocks + QUARTER) * rows, LANES), f32),
+        ),
         in_specs=[hbm] * 3,
-        out_specs=(vmem, vmem),
+        out_specs=(vmem,) * 3,
         scratch_shapes=[
             pltpu.VMEM((4, planes, *plane), f32),
             pltpu.VMEM((4, planes, *plane), f32),
+            pltpu.VMEM((4, *plane), f32),
             pltpu.VMEM((4, *plane), f32),
             *work,
             pltpu.VMEM(halo, f32),
@@ -419,11 +542,16 @@
     outs = pl.pallas_call(
         last_kernel,
         out_shape=(pltpu.HBM((planes, *plane), f32), pltpu.HBM((2, planes, *plane), f32), pltpu.HBM((planes, *plane), f32)),
-        in_specs=[vmem] * 2,
+        in_specs=[vmem] * 3,
         out_specs=(hbm,) * 3,
-        scratch_shapes=[pltpu.VMEM((4, *plane), f32), *work, pltpu.SemaphoreType.DMA((4, planes))],
+        scratch_shapes=[
+            pltpu.VMEM(half_plane, f32),
+            *work,
+            pltpu.SemaphoreType.DMA((4, planes - 1)),
+            pltpu.SemaphoreType.DMA((4, 3)),
+        ],
         compiler_params=pltpu.CompilerParams(vmem_limit_bytes=16 * 2**20),
-    )(*(pltpu.with_memory_space_constraint(a, pltpu.VMEM) for a in (done, left)))
+    )(*(pltpu.with_memory_space_constraint(a, pltpu.VMEM) for a in middle))
     return tuple(unblocked(a) for a in outs)
 
 

time: 44.6 us -> 43.9 us (0.984)
  Pallas kernels: 43.9 us -> 43.2 us
    pallas_call x1, Pallas kernels: 2.74 us -> 1.97 us  [on_device(): pl.pallas_call(last_kernel, out_shape=(pltpu.HBM((planes, *plane), f32),...]
where the time goes in v4:
time: 43.9 us; the launch traced here: 43.8 us
  Pallas kernels  43.2 us (98%)
  between operations  0.64 us (1%)
    pallas_call x1, Pallas kernels, on_device(): pl.pallas_call(kernel, out_shape=(pltpu.VMEM((4, planes - 1, *plane), f32...  41.2 us
    pallas_call x1, Pallas kernels, on_device(): pl.pallas_call(last_kernel, out_shape=(pltpu.HBM((planes, *plane), f32),...  1.97 us

profile of v4, /device:TPU:96, one launch (start us, length us, event | category | flops | bytes accessed | tf_op | source)
XLA Modules:
  0.0 43.8 jit_solution(18216919331122939763)
XLA Ops:
  0.6 41.2 %shard_map.58 = (f32[4,3,256,128]{3,2,1,0:T(8,128)S(1)}, f32[4,128,128]{2,1,0:T(8,128)S(1)}, f32[4,320,128]{2,1,0:T(8,128)S(1)}) custom-call(f32[4,256,128]{2,1,0:T(8,128)} %bitcast.31, f32[2,4,256,128]{3,2,1,0:T(8,128)} %bitcast.30, f32[4,256,128]{2,1,0:T(8,128)} %bitcast.32), custom_call_target="tpu_custom_call" | custom-call | tf_op jit(solution)/shard_map/pallas_call | solution.py:514
  41.8 2.0 %shard_map.59 = (f32[4,256,128]{2,1,0:T(8,128)}, f32[2,4,256,128]{3,2,1,0:T(8,128)}, f32[4,256,128]{2,1,0:T(8,128)}) custom-call(f32[4,3,256,128]{3,2,1,0:T(8,128)S(1)} %get-tuple-element.9.done, f32[4,128,128]{2,1,0:T(8,128)S(1)} %get-tuple-element.10.done_half, f32[4,320,128]{2,1,0:T(8,128)S(1)} %get-tuple-element.11.left), custom_call_target="tpu_custom_call" | custom-call | tf_op jit(solution)/shard_map/pallas_call | solution.py:542

commit v5 on v4

--- a/solution.py
+++ b/solution.py
@@ -211,7 +211,7 @@
 
 def kernel(
     density, velocity, pressure, done, done_half, left,
-    start, first, mid, outer, turned, swept, to_up, to_down, from_up, from_down,
+    start, first, mid, outer, turned, swept, seam, to_up, to_down, from_up, from_down,
     in_sem, send_sem, recv_sem, ready_sem,
 ):
     slab = lax.axis_index("slab")
@@ -339,19 +339,20 @@
         def _():
             send(copy_down, plane)
 
-        @pl.when(jnp.logical_and(plane == 1, place == 0))
+        @pl.when(jnp.logical_and(plane > 0, place == 0))
         def _():
             send(copy_up, plane)
 
-        @pl.when(jnp.logical_and(plane == 0, place == 0))
+        @pl.when(jnp.logical_and(plane == 2, place == 0))
         def _():
             pl.semaphore_wait(ready_sem, 1)
             send(copy_down, 0)
             send(copy_down, 1)
 
-        @pl.when(jnp.logical_and(plane > 1, place == 0))
-        def _():
-            messages(plane, both)
+        @pl.when(jnp.logical_and(plane == 3, place == 0))
+        def _():
+            send(copy_down, 2)
+            send(copy_down, 3)
 
         return carry
 
@@ -377,38 +378,60 @@
                     from_down[quarter, f * HALO + row] = outer[f, line(quarter, row)]
                     from_up[quarter, f * HALO + row] = outer[f, line(quarter, HALO + row)]
 
-    def row_sweep(plane, quarter, ref, place):
+    low = ROWS - HALO
+
+    def own_rows(f, plane, quarter, begin, end):
+        return [first[f, plane, line(quarter, row)][None] for row in range(begin, end)]
+
+    def finish_rows(cells, change, ref, place, begin):
+        for f, value in zip((0, 2, 1, 3), updated(cells, change)):
+            for row in range(value.shape[0]):
+                ref[f, line(place, begin + row)] = value[row]
+
+    def low_rows(plane, quarter, ref, place):
         unit = plane * quarters + quarter
         sides, cells = [], []
         for f in (0, 2, 1, 3):
-            own = [first[f, plane, line(quarter, row)][None] for row in range(ROWS)]
-            below = from_down[unit, pl.ds(f * HALO, HALO)]
-            above = from_up[unit, pl.ds(f * HALO, HALO)]
-            sides.append(edges(jnp.concatenate([below, *own, above], axis=0)))
-            cells.append(jnp.concatenate(own, axis=0))
+            own = own_rows(f, plane, quarter, 0, ROWS)
+            sides.append(edges(jnp.concatenate([from_down[unit, pl.ds(f * HALO, HALO)], *own], axis=0)))
+            cells.append(jnp.concatenate(own[:low], axis=0))
         flux = fluxes([s[0] for s in sides], [s[1] for s in sides], 0.05)
-        new = updated(cells, [now[1:] - now[:-1] for now in flux])
-        for f, value in zip((0, 2, 1, 3), new):
-            for row in range(ROWS):
-                ref[f, line(place, row)] = value[row]
+        finish_rows(cells, [now[1:] - now[:-1] for now in flux], ref, place, 0)
+        for f, now in enumerate(flux):
+            seam[place, f] = now[low]
+
+    def high_rows(plane, quarter, ref, place):
+        unit = plane * quarters + quarter
+        sides, cells = [], []
+        for f in (0, 2, 1, 3):
+            own = own_rows(f, plane, quarter, HALO, ROWS)
+            sides.append(edges(jnp.concatenate([*own, from_up[unit, pl.ds(f * HALO, HALO)]], axis=0)))
+            cells.append(jnp.concatenate(own[low - HALO :], axis=0))
+        flux = fluxes([s[0] for s in sides], [s[1] for s in sides], 0.05)
+        change = [now - jnp.concatenate([seam[place, f][None], now[:-1]], axis=0) for f, now in enumerate(flux)]
+        finish_rows(cells, change, ref, place, low)
 
     def later(plane, carry):
         pl.when(plane == 0)(outer_sweep)
 
-        def row_sweeps(quarter, inner):
-            @pl.when(jnp.logical_and(plane > 0, lax.rem(quarter, 2) == 0))
-            def _():
-                arrive(plane * quarters + quarter, 2)
-
-            row_sweep(plane, quarter, mid, quarter)
-            return inner
-
-        lax.fori_loop(0, quarters, row_sweeps, 0)
+        def rows_of(part, copy):
+            def one(quarter, inner):
+                @pl.when(jnp.logical_and(plane > 0, lax.rem(quarter, 2) == 0))
+                def _():
+                    copy(plane * quarters + quarter, 2).wait_recv()
+
+                part(plane, quarter, mid, quarter)
+                return inner
+
+            lax.fori_loop(0, quarters, one, 0)
+
+        rows_of(low_rows, copy_up)
+        rows_of(high_rows, copy_down)
         column_sweep(half(mid), into(done, plane), turned, swept, 0.025)
 
-        @pl.when(jnp.logical_and(place == GROUP - 1, plane + 2 >= 2))
-        def _():
-            pl.when(plane < planes - 2)(lambda: send(copy_up, plane + 2))
+        @pl.when(jnp.logical_and(place == GROUP - 1, plane < planes - 2))
+        def _():
+            send(copy_up, plane + 2)
 
         return carry
 
@@ -418,23 +441,25 @@
     def put(f, value):
         done_half[f] = value
 
-    def last_rows(step, carry):
+    def last_low(step, carry):
         quarter = last_order(step)
-        arrive(last * quarters + quarter, 1)
-        row_sweep(last, quarter, left, step)
-
-        @pl.when(step == 0)
-        def _():
-            for f in range(4):
-                left[f, pl.ds(quarters * QUARTER * ROWS, QUARTER * ROWS)] = left[f, pl.ds(0, QUARTER * ROWS)]
-
-        @pl.when(step == quarters - 2)
-        def _():
-            half_sweep(left, LEAD, put, turned, swept, 0.025)
-
+        copy_up(last * quarters + quarter, 1).wait_recv()
+        low_rows(last, quarter, left, step)
         return carry
 
-    lax.fori_loop(0, quarters, last_rows, 0)
+    def last_high(step, carry):
+        quarter = last_order(step)
+        copy_down(last * quarters + quarter, 1).wait_recv()
+        high_rows(last, quarter, left, step)
+        return carry
+
+    lax.fori_loop(0, quarters - 1, last_low, 0)
+    lax.fori_loop(0, quarters - 1, last_high, 0)
+    for f in range(4):
+        left[f, pl.ds(quarters * QUARTER * ROWS, QUARTER * ROWS)] = left[f, pl.ds(0, QUARTER * ROWS)]
+    last_low(quarters - 1, 0)
+    half_sweep(left, LEAD, put, turned, swept, 0.025)
+    last_high(quarters - 1, 0)
 
     def sent(unit, n):
         copy_up(unit, n).wait_send()
@@ -456,8 +481,8 @@
             new_velocity.at[1, plane, part], new_pressure.at[plane, part],
         )[f]
 
-    def store(plane, f):
-        return pltpu.make_async_copy(done.at[f, plane], target(plane, f, 0, total), out_sem.at[f, plane])
+    def store(f):
+        return pltpu.make_async_copy(done.at[f], target(pl.ds(0, planes), f, 0, total), out_sem.at[f])
 
     wrap = LEAD * ROWS
 
@@ -470,8 +495,7 @@
         return pltpu.make_async_copy(source, target(planes, f, first, n), half_sem.at[f, part])
 
     for f in range(4):
-        for plane in range(planes):
-            store(plane, f).start()
+        store(f).start()
         store_half(f, 0).start()
         store_half(f, 1).start()
 
@@ -481,8 +505,7 @@
 
     half_sweep(left, LEAD + LANES // ROWS, put, turned, swept, 0.025)
     for f in range(4):
-        for plane in range(planes):
-            store(plane, f).wait()
+        store(f).wait()
         for part in range(3):
             store_half(f, part).wait()
 
@@ -526,6 +549,7 @@
             pltpu.VMEM((4, *plane), f32),
             pltpu.VMEM((4, *plane), f32),
             *work,
+            pltpu.VMEM((blocks // QUARTER, 4, QUARTER, LANES), f32),
             pltpu.VMEM(halo, f32),
             pltpu.VMEM(halo, f32),
             pltpu.VMEM(halo, f32),
@@ -547,7 +571,7 @@
         scratch_shapes=[
             pltpu.VMEM(half_plane, f32),
             *work,
-            pltpu.SemaphoreType.DMA((4, planes - 1)),
+            pltpu.SemaphoreType.DMA((4,)),
             pltpu.SemaphoreType.DMA((4, 3)),
         ],
         compiler_params=pltpu.CompilerParams(vmem_limit_bytes=16 * 2**20),

time: 43.9 us -> 43.8 us (level)
  no operation moved by 1% of the time
where the time goes in v5:
time: 43.8 us; the launch traced here: 43.6 us
  Pallas kernels  42.9 us (98%)
  between operations  0.64 us (1%)
    pallas_call x1, Pallas kernels, on_device(): pl.pallas_call(kernel, out_shape=(pltpu.VMEM((4, planes - 1, *plane), f32...  41 us
    pallas_call x1, Pallas kernels, on_device(): pl.pallas_call(last_kernel, out_shape=(pltpu.HBM((planes, *plane), f32),...  1.9 us

profile of v5, /device:TPU:96, one launch (start us, length us, event | category | flops | bytes accessed | tf_op | source)
XLA Modules:
  0.0 43.6 jit_solution(3503557204070128969)
XLA Ops:
  0.6 41.0 %shard_map.58 = (f32[4,3,256,128]{3,2,1,0:T(8,128)S(1)}, f32[4,128,128]{2,1,0:T(8,128)S(1)}, f32[4,320,128]{2,1,0:T(8,128)S(1)}) custom-call(f32[4,256,128]{2,1,0:T(8,128)} %bitcast.31, f32[2,4,256,128]{3,2,1,0:T(8,128)} %bitcast.30, f32[4,256,128]{2,1,0:T(8,128)} %bitcast.32), custom_call_target="tpu_custom_call" | custom-call | tf_op jit(solution)/shard_map/pallas_call | solution.py:537
  41.7 1.9 %shard_map.59 = (f32[4,256,128]{2,1,0:T(8,128)}, f32[2,4,256,128]{3,2,1,0:T(8,128)}, f32[4,256,128]{2,1,0:T(8,128)}) custom-call(f32[4,3,256,128]{3,2,1,0:T(8,128)S(1)} %get-tuple-element.9.done, f32[4,128,128]{2,1,0:T(8,128)S(1)} %get-tuple-element.10.done_half, f32[4,320,128]{2,1,0:T(8,128)S(1)} %get-tuple-element.11.left), custom_call_target="tpu_custom_call" | custom-call | tf_op jit(solution)/shard_map/pallas_call | solution.py:566

commit v6 on v5

--- a/solution.py
+++ b/solution.py
@@ -258,10 +258,15 @@
         return (step + quarters - 1) % quarters
 
     def messages(plane, act):
-        @pl.when(plane < planes - 1)
+        @pl.when(plane < planes - 2)
         def _():
             for quarter in range(0, quarters, 2):
                 act(plane * quarters + quarter, 2)
+
+        @pl.when(jnp.logical_and(plane >= planes - 2, plane < planes - 1))
+        def _():
+            for quarter in range(quarters):
+                act(plane * quarters + quarter, 1)
 
         @pl.when(plane == planes - 1)
         def _():
@@ -416,9 +421,13 @@
 
         def rows_of(part, copy):
             def one(quarter, inner):
-                @pl.when(jnp.logical_and(plane > 0, lax.rem(quarter, 2) == 0))
+                @pl.when(jnp.logical_and(jnp.logical_and(plane > 0, plane < planes - 2), lax.rem(quarter, 2) == 0))
                 def _():
                     copy(plane * quarters + quarter, 2).wait_recv()
+
+                @pl.when(plane >= planes - 2)
+                def _():
+                    copy(plane * quarters + quarter, 1).wait_recv()
 
                 part(plane, quarter, mid, quarter)
                 return inner

time: 43.8 us -> 43.5 us (level)
  no operation moved by 1% of the time
where the time goes in v6:
time: 43.5 us; the launch traced here: 43.4 us
  Pallas kernels  42.8 us (98%)
  between operations  0.64 us (1%)
    pallas_call x1, Pallas kernels, on_device(): pl.pallas_call(kernel, out_shape=(pltpu.VMEM((4, planes - 1, *plane), f32...  40.9 us
    pallas_call x1, Pallas kernels, on_device(): pl.pallas_call(last_kernel, out_shape=(pltpu.HBM((planes, *plane), f32),...  1.9 us

profile of v6, /device:TPU:96, one launch (start us, length us, event | category | flops | bytes accessed | tf_op | source)
XLA Modules:
  0.0 43.4 jit_solution(3984913490743103454)
XLA Ops:
  0.6 40.9 %shard_map.58 = (f32[4,3,256,128]{3,2,1,0:T(8,128)S(1)}, f32[4,128,128]{2,1,0:T(8,128)S(1)}, f32[4,320,128]{2,1,0:T(8,128)S(1)}) custom-call(f32[4,256,128]{2,1,0:T(8,128)} %bitcast.31, f32[2,4,256,128]{3,2,1,0:T(8,128)} %bitcast.30, f32[4,256,128]{2,1,0:T(8,128)} %bitcast.32), custom_call_target="tpu_custom_call" | custom-call | tf_op jit(solution)/shard_map/pallas_call | solution.py:546
  41.5 1.9 %shard_map.59 = (f32[4,256,128]{2,1,0:T(8,128)}, f32[2,4,256,128]{3,2,1,0:T(8,128)}, f32[4,256,128]{2,1,0:T(8,128)}) custom-call(f32[4,3,256,128]{3,2,1,0:T(8,128)S(1)} %get-tuple-element.9.done, f32[4,128,128]{2,1,0:T(8,128)S(1)} %get-tuple-element.10.done_half, f32[4,320,128]{2,1,0:T(8,128)S(1)} %get-tuple-element.11.left), custom_call_target="tpu_custom_call" | custom-call | tf_op jit(solution)/shard_map/pallas_call | solution.py:575

commit v7 on v6

--- a/solution.py
+++ b/solution.py
@@ -273,8 +273,8 @@
             for step in range(quarters):
                 act(plane * quarters + last_order(step), 1)
 
-    def pack(ref, plane):
-        for quarter in range(quarters):
+    def pack(ref, plane, begin=0, end=quarters):
+        for quarter in range(begin, end):
             unit = plane * quarters + quarter
             for f in range(4):
                 for row in range(HALO):
@@ -286,8 +286,7 @@
 
     for f in range(4):
         load(0, f).wait()
-    load_all(1)
-    pack(start, 0)
+    pack(start, 0, 0, 2)
 
     @pl.when(place == 0)
     def _():
@@ -302,18 +301,21 @@
         pl.semaphore_signal(ready_sem, inc=1, device_id=(slab, up), device_id_type=MESH)
 
     ahead = place == GROUP - 1
-
-    @pl.when(ahead)
-    def _():
-        send(copy_down, 0)
-
-    send(copy_up, 0)
-
-    @pl.when(jnp.logical_and(place > 0, jnp.logical_not(ahead)))
-    def _():
-        send(copy_down, 0)
-
-    for plane in range(2, planes):
+    for unit in range(0, quarters, 2):
+        if unit:
+            pack(start, 0, unit, unit + 2)
+
+        @pl.when(ahead)
+        def _():
+            copy_down(unit, 2).start()
+
+        copy_up(unit, 2).start()
+
+        @pl.when(jnp.logical_and(place > 0, jnp.logical_not(ahead)))
+        def _():
+            copy_down(unit, 2).start()
+
+    for plane in range(1, planes):
         load_all(plane)
 
     def first_sweep(step, carry):

time: 43.5 us -> 43.6 us (level)
  no operation moved by 1% of the time
where the time goes in v7:
time: 43.6 us; the launch traced here: 43.4 us
  Pallas kernels  42.7 us (98%)
  between operations  0.64 us (1%)
    pallas_call x1, Pallas kernels, on_device(): pl.pallas_call(kernel, out_shape=(pltpu.VMEM((4, planes - 1, *plane), f32...  40.8 us
    pallas_call x1, Pallas kernels, on_device(): pl.pallas_call(last_kernel, out_shape=(pltpu.HBM((planes, *plane), f32),...  1.9 us

profile of v7, /device:TPU:96, one launch (start us, length us, event | category | flops | bytes accessed | tf_op | source)
XLA Modules:
  0.0 43.4 jit_solution(6253681975030207530)
XLA Ops:
  0.6 40.8 %shard_map.58 = (f32[4,3,256,128]{3,2,1,0:T(8,128)S(1)}, f32[4,128,128]{2,1,0:T(8,128)S(1)}, f32[4,320,128]{2,1,0:T(8,128)S(1)}) custom-call(f32[4,256,128]{2,1,0:T(8,128)} %bitcast.31, f32[2,4,256,128]{3,2,1,0:T(8,128)} %bitcast.30, f32[4,256,128]{2,1,0:T(8,128)} %bitcast.32), custom_call_target="tpu_custom_call" | custom-call | tf_op jit(solution)/shard_map/pallas_call | solution.py:548
  41.5 1.9 %shard_map.59 = (f32[4,256,128]{2,1,0:T(8,128)}, f32[2,4,256,128]{3,2,1,0:T(8,128)}, f32[4,256,128]{2,1,0:T(8,128)}) custom-call(f32[4,3,256,128]{3,2,1,0:T(8,128)S(1)} %get-tuple-element.9.done, f32[4,128,128]{2,1,0:T(8,128)S(1)} %get-tuple-element.10.done_half, f32[4,320,128]{2,1,0:T(8,128)S(1)} %get-tuple-element.11.left), custom_call_target="tpu_custom_call" | custom-call | tf_op jit(solution)/shard_map/pallas_call | solution.py:577
